TPU v7x, 32 devices: a whole 2x2x4 slice. The times are simulated.
32 devices in a mesh: shift: 4 (over y, x), rows: 8 (over z, core).
Axes of the slice: x: 2, y: 2, z: 4, core: 2. Of those that a mesh axis runs over, the one named last changes fastest.
Arguments:
- zc_in: bfloat16 [4, 512, 16384], P('shift', 'rows'), may hold values from -6 to 6
- zo_in: bfloat16 [4, 384, 16384], P('shift', 'rows'), may hold values from -6 to 6
- count_c: int32 [4], replicated, may hold values from 256 to 512, as said below
- count_o: int32 [4], replicated, may hold values from 192 to 384, as said below
- mass: bfloat16 [128, 4, 128, 128], P(('shift', 'rows')), may hold values from -0.25 to 0.25
- adjacency: int32 [128, 4], P(('shift', 'rows')), may hold values from 0 to 127, as said below
- ghost_len: int32 [128, 4], P(('shift', 'rows')), may hold values from 1 to 128, as said below
- omega: float32 [2048, 128], replicated, may hold values from -6 to 6
Outputs:
- proj_c: float32 [128, 16384], P(None, ('shift', 'rows'))
- proj_o: float32 [128, 16384], P(None, ('shift', 'rows'))
Inputs may be any that keep to these rules, and one draw needn't show every extreme that they name: `count_c`: each entry is 256 or more, and one group holds 512 exactly. `count_o`: each entry is 192 or more, and one group holds 384 exactly. adjacency[i, 0] = i, and every entry lies within 2 blocks of i. ghost_len[i, 0] = 128.
All inputs are finite; a program needn't handle non-finite values.
Results may differ from a plain program's by a relative error of at most 0.0047.
Values may be sent and summed in bfloat16 or wider, within the bound.
A program may use at most 128 MiB of HBM per device.

v0:
```python
import jax
import jax.numpy as jnp
from jax import lax
from jax.sharding import PartitionSpec as P

REACH = 2


def padded(shard, sides, width):
    for axis, dim in sides:
        size, length = (lax.axis_size(axis), shard.shape[dim])
        up = [(i, (i + 1) % size) for i in range(size - 1)]
        down = [(j, i) for i, j in up]
        last = lax.slice_in_dim(shard, length - width, length, axis=dim)
        initial = lax.slice_in_dim(shard, 0, width, axis=dim)
        before = lax.ppermute(last, axis, up)
        after = lax.ppermute(initial, axis, down)
        shard = jnp.concatenate([before, shard, after], axis=dim)
    return shard


def prepare(factor, counts, group, member):
    width = factor.shape[1]
    slots = member * width + jnp.arange(width, dtype=jnp.int32)
    keep = slots < counts[group]
    return jnp.where(keep[:, None], factor[0], jnp.zeros_like(factor[0]))


def orth_local(matrix):
    square = jnp.dot(matrix.T, matrix, precision=lax.Precision.HIGHEST)
    lower = jnp.linalg.cholesky(square)
    return jax.scipy.linalg.solve_triangular(lower, matrix.T, lower=True).T


def per_device(zc_in, zo_in, count_c, count_o, mass, adjacency, ghost_len, omega):
    group = lax.axis_index("shift")
    member = lax.axis_index("rows")
    members = lax.axis_size("rows")
    part_c = prepare(zc_in, count_c, group, member)
    part_o = prepare(zo_in, count_o, group, member)
    zc, zo = (
        lax.all_to_all(part_c, ("shift", "rows"), split_axis=1, concat_axis=0, tiled=True),
        lax.all_to_all(part_o, ("shift", "rows"), split_axis=1, concat_axis=0, tiled=True),
    )
    width_c = zc.shape[0]
    rows_here = zc.shape[1]
    block_size = mass.shape[2]
    count_blocks = rows_here // block_size
    extended = padded(zc, ((("shift", "rows"), 1),), REACH * block_size)
    first_block = (group * members + member) * count_blocks
    local_index = (adjacency - first_block + REACH).reshape(-1)
    blocks = extended.reshape(width_c, count_blocks + 2 * REACH, block_size)
    pieces = jnp.take(blocks, local_index, axis=1).reshape(
        width_c, count_blocks, adjacency.shape[1], block_size
    )
    inner = jnp.arange(block_size, dtype=jnp.int32)
    keep = inner[None, None, None, :] < ghost_len[:, :, None, None]
    masked = jnp.where(keep, mass, jnp.zeros_like(mass))
    mixed = jnp.einsum("cikp,ikqp->ciq", pieces, masked, preferred_element_type=jnp.float32)
    mixed = mixed.astype(jnp.bfloat16).reshape(width_c, rows_here)
    high = lax.Precision.HIGHEST
    partial_gram = lax.dot_general(
        zo, mixed, (((1,), (1,)), ((), ())), preferred_element_type=jnp.float32
    )
    gram = lax.psum(partial_gram, ("shift", "rows"))
    first = orth_local(jnp.dot(gram, omega, precision=high))
    right = orth_local(jnp.dot(gram.T, first, precision=high))
    left = orth_local(jnp.dot(gram, right, precision=high))
    proj_c = jnp.dot(right.astype(jnp.bfloat16).T, zc, preferred_element_type=jnp.float32)
    proj_o = jnp.dot(left.astype(jnp.bfloat16).T, zo, preferred_element_type=jnp.float32)
    return (proj_c, proj_o)


def solution(mesh):
    placed = (
        P("shift", "rows", None),
        P("shift", "rows", None),
        P(),
        P(),
        P(("shift", "rows"), None, None, None),
        P(("shift", "rows"), None),
        P(("shift", "rows"), None),
        P(),
    )
    return jax.shard_map(
        per_device,
        mesh=mesh,
        in_specs=placed,
        out_specs=(P(None, ("shift", "rows")), P(None, ("shift", "rows"))),
        check_vma=False,
    )
```

profile of v0, /device:TPU:0, one launch (start us, length us, event | category | flops | bytes accessed | tf_op | source)
XLA Modules:
  0.0 544.3 jit_solution(15689129905431404123)
XLA Ops:
  7.2 0.0 copy-start
  7.2 0.0 copy-start.5
  7.2 2.4 copy.32
  9.6 0.0 copy-done.5
  9.7 0.6 dynamic_slice.7
  10.2 0.7 add_compare_fusion
  10.9 0.4 bitcast_select_fusion
  11.3 0.0 copy-start.6
  11.3 2.5 copy.24
  13.8 7.3 %all-to-all-start.1 = ((bf16[64,32,512]{2,0,1:T(8,128)(2,1)}), bf16[64,32,512]{2,0,1:T(8,128)(2,1)S(1)}, u32[]{:S(2)}, u32[]{:S(2)}) async-start(bf16[64,32,512]{2,0,1:T(8,128)(2,1)} %copy.24), calls=%async_computation.1 | async-start | bytes 4194304 | tf_op jit(solution)/shard_map/all_to_all | solution.py:42
  21.1 0.6 dynamic_slice.6
  21.7 2.0 copy.31
  23.7 0.7 add_compare_fusion.1
  24.3 0.3 bitcast_select_fusion.1
  24.6 2.1 copy.23
  26.7 44.5 %all-to-all-done.1 = bf16[64,32,512]{2,0,1:T(8,128)(2,1)S(1)} async-done(((bf16[64,32,512]{2,0,1:T(8,128)(2,1)}), bf16[64,32,512]{2,0,1:T(8,128)(2,1)S(1)}, u32[]{:S(2)}, u32[]{:S(2)}) %all-to-all-start.1) | async-done | bytes 2097184 | tf_op jit(solution)/shard_map/all_to_all | solution.py:42
  71.2 3.4 all-to-all-start
  74.6 0.0 all-reduce.2.cloned.1.call-start
  74.7 1.5 fusion.29
  76.2 3.0 collective-permute-start
  79.1 1.5 collective-permute-start.1
  80.6 0.0 copy-done.3
  80.6 0.1 reshape.99
  80.8 0.1 iota_compare_fusion.2
  80.8 0.0 collective-permute-done
  80.8 3.4 collective-permute-done.1
  84.2 3.4 pad_maximum_fusion
  87.6 6.5 %copy.25 = bf16[2048,1024]{0,1:T(8,128)(2,1)} copy(bf16[2048,1024]{1,0:T(8,128)(2,1)} %pad_maximum_fusion) | data formatting | bytes 8388608 | tf_op jit(solution)/shard_map/concatenate | solution.py:18
  94.1 6.5 %copy.26 = bf16[2048,8,128]{2,0,1:T(8,128)(2,1)} copy(bf16[2048,8,128]{0,2,1:T(8,128)(2,1)} %bitcast.82) | data formatting | bytes 8388608 | tf_op jit(solution)/shard_map/reshape | solution.py:52
  100.6 6.9 %gather_fusion = bf16[16,2048,128]{2,1,0:T(8,128)(2,1)} fusion(bf16[2048,8,128]{2,0,1:T(8,128)(2,1)} %copy.26, s32[1024]{0:T(1024)S(1)} %pad_clamp_fusion), kind=kCustom, calls=%fused_computation | custom fusion | bytes 16777280 | tf_op jit(solution)/shard_map/jit(_take)/gather | solution.py:53
  107.5 7.8 %bitcast_convert_fusion = bf16[4,128,2048]{2,1,0:T(8,128)(2,1)} fusion(bf16[2048,4,4,128]{3,0,2,1:T(8,128)(2,1)} %bitcast.83, pred[4,4]{1,0:T(4,128)(4,1)S(1)} %compare_and_fusion, bf16[4,4,128,128]{3,2,1,0:T(8,128)(2,1)} %param.15, pred[4,4,128]{2,1,0:T(4,128)(4,1)S(1)} %iota_compare_fusion.2), kind=kOutput, calls=%fused_computation.5 | convolution fusion | flops 1079246848 | bytes 11012112 | tf_op jit(solution)/shard_map/cikp,ikqp->ciq/dot_general | solution.py:59
  115.3 0.0 all-to-all-done
  115.3 10.0 %fusion.30 = f32[1536,2048]{1,0:T(8,128)} fusion(bf16[1536,512]{1,0:T(8,128)(2,1)} %bitcast.2, bf16[2048,512]{0,1:T(8,128)(2,1)} %bitcast.86), kind=kOutput, calls=%fused_computation.55 | convolution fusion | flops 3221225472 | bytes 16252928 | tf_op jit(solution)/shard_map/dot_general | solution.py:62
  125.3 0.0 all-reduce.2.cloned.1.call-update
  125.4 278.8 %all-reduce.2.cloned.1.call-done = f32[1536,2048]{1,0:T(8,128)} async-done(((f32[1536,2048]{1,0:T(8,128)}), f32[1536,2048]{1,0:T(8,128)}) %all-reduce.2.cloned.1.call-update) | async-done | bytes 12582928 | tf_op jit(solution)/shard_map/psum | solution.py:65
  404.1 0.0 copy-done
  404.1 12.7 %fusion.31 = f32[1536,128]{1,0:T(8,128)S(1)} fusion(f32[1536,2048]{1,0:T(8,128)} %all-reduce.2.cloned.1.call-done, f32[2048,128]{1,0:T(8,128)S(1)} %copy-done), kind=kOutput, calls=%fused_computation.56 | convolution fusion | flops 4831838208 | bytes 14417920 | tf_op jit(solution)/shard_map/dot_general | solution.py:66
  416.8 0.9 copy-done.2
  417.8 1.5 fusion.32
  419.2 0.1 copy.27
  419.3 11.7 %cholesky.59 = f32[128,128]{1,0:T(8,128)S(1)} custom-call(f32[128,128]{1,0:T(8,128)S(1)} %fusion.23), custom_call_target="Cholesky" | custom-call | tf_op jit(solution)/shard_map/jit(cholesky)/cholesky | solution.py:31
  431.1 0.6 compare_reduce_fusion.2
  431.7 0.7 fusion.14
  432.4 9.8 %custom-call.11 = f32[1,128,128]{1,2,0:T(8,128)S(1)} custom-call(f32[1,128,128]{2,1,0:T(8,128)S(1)} %fusion.14), custom_call_target="InvertDiagBlocksLowerTriangular" | custom-call | tf_op jit(solution)/shard_map/jit(_solve_triangular)/triangular_solve | solution.py:32
  442.2 2.0 fusion.7
  444.2 23.2 %fusion.33 = f32[2048,128]{1,0:T(8,128)S(1)} fusion(f32[1536,2048]{1,0:T(8,128)} %all-reduce.2.cloned.1.call-done, f32[128,1536]{1,0:T(8,128)S(1)} %fusion.7), kind=kOutput, calls=%fused_computation.58 | convolution fusion | flops 4831838208 | bytes 14417920 | tf_op jit(solution)/shard_map/dot_general | solution.py:67
  467.4 1.0 copy-done.1
  468.5 1.9 fusion.34
  470.4 0.1 copy.28
  470.5 11.7 %cholesky.70 = f32[128,128]{1,0:T(8,128)S(1)} custom-call(f32[128,128]{1,0:T(8,128)S(1)} %fusion.21), custom_call_target="Cholesky" | custom-call | tf_op jit(solution)/shard_map/jit(cholesky)/cholesky | solution.py:31
  482.2 0.6 compare_reduce_fusion.1
  482.9 0.7 fusion.15
  483.5 9.8 %custom-call.9 = f32[1,128,128]{1,2,0:T(8,128)S(1)} custom-call(f32[1,128,128]{2,1,0:T(8,128)S(1)} %fusion.15), custom_call_target="InvertDiagBlocksLowerTriangular" | custom-call | tf_op jit(solution)/shard_map/jit(_solve_triangular)/triangular_solve | solution.py:32
  493.3 2.3 fusion.19
  495.6 1.2 fusion.9
  496.8 12.7 %fusion.35 = f32[1536,128]{1,0:T(8,128)S(1)} fusion(f32[1536,2048]{1,0:T(8,128)} %all-reduce.2.cloned.1.call-done, f32[128,2048]{1,0:T(8,128)S(1)} %fusion.19), kind=kOutput, calls=%fused_computation.60 | convolution fusion | flops 4831838208 | bytes 14417920 | tf_op jit(solution)/shard_map/dot_general | solution.py:68
  509.5 1.4 fusion.36
  510.9 0.1 copy.29
  511.0 11.7 %cholesky.81 = f32[128,128]{1,0:T(8,128)S(1)} custom-call(f32[128,128]{1,0:T(8,128)S(1)} %fusion.18), custom_call_target="Cholesky" | custom-call | tf_op jit(solution)/shard_map/jit(cholesky)/cholesky | solution.py:31
  522.8 0.6 compare_reduce_fusion
  523.4 0.7 fusion.16
  524.1 9.8 %custom-call.12 = f32[1,128,128]{1,2,0:T(8,128)S(1)} custom-call(f32[1,128,128]{2,1,0:T(8,128)S(1)} %fusion.16), custom_call_target="InvertDiagBlocksLowerTriangular" | custom-call | tf_op jit(solution)/shard_map/jit(_solve_triangular)/triangular_solve | solution.py:32
  533.9 0.9 convolution_convert_fusion
  534.8 2.5 fusion.37
  (16 shorter events, 0.2 us)
Async XLA Ops:
  7.2 397.0 %copy-start = (f32[2048,128]{1,0:T(8,128)S(1)}, f32[2048,128]{1,0:T(8,128)}, u32[]{:S(2)}) copy-start(f32[2048,128]{1,0:T(8,128)} %param.18) | copy-start | bytes 3145732
  7.2 2.5 copy-start.5
  11.3 9.8 %copy-start.6 = (s32[4]{0:T(128)S(1)}, s32[4]{0:T(128)}, u32[]{:S(2)}) copy-start(s32[4]{0:T(128)} %param.14) | copy-start | bytes 52
  13.8 57.4 %all-to-all-start.1 = ((bf16[64,32,512]{2,0,1:T(8,128)(2,1)}), bf16[64,32,512]{2,0,1:T(8,128)(2,1)S(1)}, u32[]{:S(2)}, u32[]{:S(2)}) async-start(bf16[64,32,512]{2,0,1:T(8,128)(2,1)} %copy.24), calls=%async_computation.1 | async-start | bytes 4194304 | tf_op jit(solution)/shard_map/all_to_all | solution.py:42
  26.7 53.9 %copy-start.3 = (s32[4,4]{1,0:T(4,128)S(1)}, s32[4,4]{1,0:T(4,128)}, u32[]{:S(2)}) copy-start(s32[4,4]{1,0:T(4,128)} %param.16) | copy-start | bytes 196
  26.7 54.0 %copy-start.4 = (s32[4,4]{1,0:T(4,128)S(1)}, s32[4,4]{1,0:T(4,128)}, u32[]{:S(2)}) copy-start(s32[4,4]{1,0:T(4,128)} %param.17) | copy-start | bytes 196
  71.2 44.1 %all-to-all-start = ((bf16[48,32,512]{2,0,1:T(8,128)(2,1)}), bf16[48,32,512]{2,0,1:T(8,128)(2,1)}, u32[]{:S(2)}, u32[]{:S(2)}) async-start(bf16[48,32,512]{2,0,1:T(8,128)(2,1)} %copy.23), calls=%async_computation | async-start | bytes 3145728 | tf_op jit(solution)/shard_map/all_to_all | solution.py:43
  74.6 329.5 %all-reduce.2.cloned.1.call-start = ((), (), s32[]{:S(2)}) async-start(), calls=%async_computation.2 | async-start | bytes 25165824 | tf_op jit(solution)/shard_map/psum | solution.py:65
  76.2 4.7 collective-permute-start
  79.1 5.1 collective-permute-start.1
  416.8 0.9 copy-start.2
  467.4 1.1 copy-start.1
Sparse Core Ops, SparseCore 0:
  125.5 278.5 all-reduce.1
where the time goes:
time: 549 us; the launch traced here: 544 us
  waiting for transfers between devices  327 us (60%)
  matrix products  80 us (15%)
  other arithmetic  74.1 us (13%)
  local copies, waits for them, and re-layouts  33.9 us (6%)
  starting transfers between devices  15.2 us (3%)
  between operations  14.6 us (3%)
    psum x1, waiting for transfers between devices, per_device(): gram = lax.psum(partial_gram, ('shift', 'rows'))  279 us
    all_to_all x1, waiting for transfers between devices, per_device(): lax.all_to_all(part_c, ('shift', 'rows'), split_axis=1, concat_axis=0, ti...  44.5 us
    another operation x9, other arithmetic, orth_local(): lower = jnp.linalg.cholesky(square)  37.2 us
    another operation x6, other arithmetic, orth_local(): return jax.scipy.linalg.solve_triangular(lower, matrix.T, lower=True).T  31.4 us
    dot_general x1, matrix products, per_device(): right = orth_local(jnp.dot(gram.T, first, precision=high))  23.2 us
    dot_general x1, matrix products, per_device(): first = orth_local(jnp.dot(gram, omega, precision=high))  12.7 us
    dot_general x1, matrix products, per_device(): left = orth_local(jnp.dot(gram, right, precision=high))  12.7 us
  transfers between devices with their start and end apart: 5, of which 3 were waited for; matrix products, arithmetic and copies ran while one was open for 7% of the time, Pallas kernels for 0%

commit v1 on v0

--- a/solution.py
+++ b/solution.py
@@ -2,6 +2,7 @@
 import jax.numpy as jnp
 from jax import lax
 from jax.sharding import PartitionSpec as P
+from jax.lax import psum
 
 REACH = 2
 
@@ -62,7 +63,9 @@
     partial_gram = lax.dot_general(
         zo, mixed, (((1,), (1,)), ((), ())), preferred_element_type=jnp.float32
     )
-    gram = lax.psum(partial_gram, ("shift", "rows"))
+    gram = partial_gram
+    for rr in ("rows", "shift"):
+        gram = psum(gram, axis_name=rr)
     first = orth_local(jnp.dot(gram, omega, precision=high))
     right = orth_local(jnp.dot(gram.T, first, precision=high))
     left = orth_local(jnp.dot(gram, right, precision=high))

time: 549 us -> 821 us (1.50)
  waiting for transfers between devices: 327 us -> 595 us
    psum x1 -> x2, waiting for transfers between devices: 279 us -> 546 us  [per_device(): gram = psum(gram, axis_name=rr)]
  transfers between devices with their start and end apart: 5 -> 6, of which waited for: 3 -> 5; matrix products, arithmetic and copies ran while one was open for 7% -> 5% of each run, Pallas kernels for 0% -> 0%
where the time goes in v1:
time: 821 us; the launch traced here: 812 us
  waiting for transfers between devices  595 us (72%)
  matrix products  79.9 us (10%)
  other arithmetic  74.1 us (9%)
  local copies, waits for them, and re-layouts  33.8 us (4%)
  starting transfers between devices  15 us (2%)
  between operations  14.5 us (2%)
    psum x2, waiting for transfers between devices, per_device(): gram = psum(gram, axis_name=rr)  546 us
    all_to_all x1, waiting for transfers between devices, per_device(): lax.all_to_all(part_c, ('shift', 'rows'), split_axis=1, concat_axis=0, ti...  44.5 us
    another operation x9, other arithmetic, orth_local(): lower = jnp.linalg.cholesky(square)  37.2 us
    another operation x6, other arithmetic, orth_local(): return jax.scipy.linalg.solve_triangular(lower, matrix.T, lower=True).T  31.4 us
    dot_general x1, matrix products, per_device(): right = orth_local(jnp.dot(gram.T, first, precision=high))  23.3 us
  transfers between devices with their start and end apart: 6, of which 5 were waited for; matrix products, arithmetic and copies ran while one was open for 5% of the time, Pallas kernels for 0%

profile of v1, /device:TPU:0, one launch (start us, length us, event | category | flops | bytes accessed | tf_op | source)
XLA Modules:
  0.0 812.0 jit_solution(13888235836365079452)
XLA Ops:
  7.2 0.0 copy-start
  7.2 0.0 copy-start.5
  7.2 2.4 copy.32
  9.7 0.6 dynamic_slice.7
  10.2 0.7 add_compare_fusion
  10.9 0.4 bitcast_select_fusion
  11.3 0.0 copy-start.6
  11.3 2.5 copy.24
  13.8 7.3 all-to-all-start.1
  21.1 0.6 dynamic_slice.6
  21.7 2.0 copy.31
  23.7 0.7 add_compare_fusion.1
  24.3 0.3 bitcast_select_fusion.1
  24.6 2.0 copy.23
  26.7 44.5 %all-to-all-done.1 = bf16[64,32,512]{2,0,1:T(8,128)(2,1)S(1)} async-done(((bf16[64,32,512]{2,0,1:T(8,128)(2,1)}), bf16[64,32,512]{2,0,1:T(8,128)(2,1)S(1)}, u32[]{:S(2)}, u32[]{:S(2)}) %all-to-all-start.1) | async-done | bytes 2097184 | tf_op jit(solution)/shard_map/all_to_all | solution.py:43
  71.2 3.4 all-to-all-start
  74.6 0.0 all-reduce.3.cloned.1.call-start
  74.7 1.5 fusion.29
  76.1 2.9 collective-permute-start
  79.1 1.3 collective-permute-start.1
  80.4 0.1 reshape.99
  80.5 0.1 iota_compare_fusion.2
  80.6 0.1 collective-permute-done
  80.7 3.5 collective-permute-done.1
  84.2 3.4 pad_maximum_fusion
  87.6 6.5 copy.25
  94.1 6.5 copy.26
  100.6 6.9 gather_fusion
  107.5 7.8 bitcast_convert_fusion
  115.3 0.0 all-to-all-done
  115.3 10.1 %fusion.30 = f32[1536,2048]{1,0:T(8,128)} fusion(bf16[1536,512]{1,0:T(8,128)(2,1)} %bitcast.2, bf16[2048,512]{0,1:T(8,128)(2,1)} %bitcast.86), kind=kOutput, calls=%fused_computation.55 | convolution fusion | flops 3221225472 | bytes 16252928 | tf_op jit(solution)/shard_map/dot_general | solution.py:63
  125.4 0.0 all-reduce.3.cloned.1.call-update
  125.4 0.0 all-reduce.5.cloned.1.call-start
  125.4 303.2 %all-reduce.3.cloned.1.call-done = f32[1536,2048]{1,0:T(8,128)} async-done(((f32[1536,2048]{1,0:T(8,128)}), f32[1536,2048]{1,0:T(8,128)}) %all-reduce.3.cloned.1.call-update) | async-done | bytes 12582928 | tf_op jit(solution)/shard_map/psum | solution.py:68
  428.6 0.0 all-reduce.5.cloned.1.call-update
  428.7 243.2 %all-reduce.5.cloned.1.call-done = f32[1536,2048]{1,0:T(8,128)} async-done(((f32[1536,2048]{1,0:T(8,128)}), f32[1536,2048]{1,0:T(8,128)}) %all-reduce.5.cloned.1.call-update) | async-done | bytes 12582928 | tf_op jit(solution)/shard_map/psum | solution.py:68
  671.9 12.6 %fusion.31 = f32[1536,128]{1,0:T(8,128)S(1)} fusion(f32[1536,2048]{1,0:T(8,128)} %all-reduce.5.cloned.1.call-done, f32[2048,128]{1,0:T(8,128)S(1)} %copy-done), kind=kOutput, calls=%fused_computation.56 | convolution fusion | flops 4831838208 | bytes 14417920 | tf_op jit(solution)/shard_map/dot_general | solution.py:69
  684.6 0.9 copy-done.2
  685.5 1.5 fusion.32
  686.9 0.1 copy.27
  687.0 11.7 %cholesky.59 = f32[128,128]{1,0:T(8,128)S(1)} custom-call(f32[128,128]{1,0:T(8,128)S(1)} %fusion.23), custom_call_target="Cholesky" | custom-call | tf_op jit(solution)/shard_map/jit(cholesky)/cholesky | solution.py:32
  698.8 0.6 compare_reduce_fusion.2
  699.4 0.7 fusion.14
  700.1 9.8 %custom-call.11 = f32[1,128,128]{1,2,0:T(8,128)S(1)} custom-call(f32[1,128,128]{2,1,0:T(8,128)S(1)} %fusion.14), custom_call_target="InvertDiagBlocksLowerTriangular" | custom-call | tf_op jit(solution)/shard_map/jit(_solve_triangular)/triangular_solve | solution.py:33
  709.9 2.0 fusion.7
  711.9 23.3 %fusion.33 = f32[2048,128]{1,0:T(8,128)S(1)} fusion(f32[1536,2048]{1,0:T(8,128)} %all-reduce.5.cloned.1.call-done, f32[128,1536]{1,0:T(8,128)S(1)} %fusion.7), kind=kOutput, calls=%fused_computation.58 | convolution fusion | flops 4831838208 | bytes 14417920 | tf_op jit(solution)/shard_map/dot_general | solution.py:70
  735.2 1.0 copy-done.1
  736.2 1.9 fusion.34
  738.1 0.1 copy.28
  738.2 11.7 %cholesky.70 = f32[128,128]{1,0:T(8,128)S(1)} custom-call(f32[128,128]{1,0:T(8,128)S(1)} %fusion.21), custom_call_target="Cholesky" | custom-call | tf_op jit(solution)/shard_map/jit(cholesky)/cholesky | solution.py:32
  750.0 0.6 compare_reduce_fusion.1
  750.6 0.7 fusion.15
  751.3 9.8 %custom-call.9 = f32[1,128,128]{1,2,0:T(8,128)S(1)} custom-call(f32[1,128,128]{2,1,0:T(8,128)S(1)} %fusion.15), custom_call_target="InvertDiagBlocksLowerTriangular" | custom-call | tf_op jit(solution)/shard_map/jit(_solve_triangular)/triangular_solve | solution.py:33
  761.1 2.3 fusion.19
  763.4 1.2 fusion.9
  764.6 12.6 %fusion.35 = f32[1536,128]{1,0:T(8,128)S(1)} fusion(f32[1536,2048]{1,0:T(8,128)} %all-reduce.5.cloned.1.call-done, f32[128,2048]{1,0:T(8,128)S(1)} %fusion.19), kind=kOutput, calls=%fused_computation.60 | convolution fusion | flops 4831838208 | bytes 14417920 | tf_op jit(solution)/shard_map/dot_general | solution.py:71
  777.2 1.4 fusion.36
  778.6 0.1 copy.29
  778.7 11.7 %cholesky.81 = f32[128,128]{1,0:T(8,128)S(1)} custom-call(f32[128,128]{1,0:T(8,128)S(1)} %fusion.18), custom_call_target="Cholesky" | custom-call | tf_op jit(solution)/shard_map/jit(cholesky)/cholesky | solution.py:32
  790.5 0.6 compare_reduce_fusion
  791.1 0.7 fusion.16
  791.8 9.8 %custom-call.12 = f32[1,128,128]{1,2,0:T(8,128)S(1)} custom-call(f32[1,128,128]{2,1,0:T(8,128)S(1)} %fusion.16), custom_call_target="InvertDiagBlocksLowerTriangular" | custom-call | tf_op jit(solution)/shard_map/jit(_solve_triangular)/triangular_solve | solution.py:33
  801.6 0.9 convolution_convert_fusion
  802.5 2.5 fusion.37
  (19 shorter events, 0.2 us)
Async XLA Ops:
  7.2 664.7 %copy-start = (f32[2048,128]{1,0:T(8,128)S(1)}, f32[2048,128]{1,0:T(8,128)}, u32[]{:S(2)}) copy-start(f32[2048,128]{1,0:T(8,128)} %param.18) | copy-start | bytes 3145732
  7.2 2.5 copy-start.5
  11.3 9.8 %copy-start.6 = (s32[4]{0:T(128)S(1)}, s32[4]{0:T(128)}, u32[]{:S(2)}) copy-start(s32[4]{0:T(128)} %param.14) | copy-start | bytes 52
  13.8 57.4 %all-to-all-start.1 = ((bf16[64,32,512]{2,0,1:T(8,128)(2,1)}), bf16[64,32,512]{2,0,1:T(8,128)(2,1)S(1)}, u32[]{:S(2)}, u32[]{:S(2)}) async-start(bf16[64,32,512]{2,0,1:T(8,128)(2,1)} %copy.24), calls=%async_computation.1 | async-start | bytes 4194304 | tf_op jit(solution)/shard_map/all_to_all | solution.py:43
  26.7 53.7 %copy-start.3 = (s32[4,4]{1,0:T(4,128)S(1)}, s32[4,4]{1,0:T(4,128)}, u32[]{:S(2)}) copy-start(s32[4,4]{1,0:T(4,128)} %param.16) | copy-start | bytes 196
  26.7 53.8 %copy-start.4 = (s32[4,4]{1,0:T(4,128)S(1)}, s32[4,4]{1,0:T(4,128)}, u32[]{:S(2)}) copy-start(s32[4,4]{1,0:T(4,128)} %param.17) | copy-start | bytes 196
  71.2 44.1 %all-to-all-start = ((bf16[48,32,512]{2,0,1:T(8,128)(2,1)}), bf16[48,32,512]{2,0,1:T(8,128)(2,1)}, u32[]{:S(2)}, u32[]{:S(2)}) async-start(bf16[48,32,512]{2,0,1:T(8,128)(2,1)} %copy.23), calls=%async_computation | async-start | bytes 3145728 | tf_op jit(solution)/shard_map/all_to_all | solution.py:44
  74.6 354.0 %all-reduce.3.cloned.1.call-start = ((), (), s32[]{:S(2)}) async-start(), calls=%async_computation.2 | async-start | bytes 25165824 | tf_op jit(solution)/shard_map/psum | solution.py:68
  76.1 4.6 collective-permute-start
  79.1 5.1 collective-permute-start.1
  125.4 546.5 %all-reduce.5.cloned.1.call-start = ((), (), s32[]{:S(2)}) async-start(), calls=%async_computation.3 | async-start | bytes 25165824 | tf_op jit(solution)/shard_map/psum | solution.py:68
  684.5 0.9 copy-start.2
  735.2 1.1 copy-start.1
Sparse Core Ops, SparseCore 0:
  125.5 303.1 all-reduce.2
  432.1 239.7 all-reduce.4
